TPU v7x, 32 devices: a whole 2x2x4 slice. The times are simulated.
32 devices in a mesh: dom: 8 (over z, x), rep: 4 (over y, core).
Axes of the slice: x: 2, y: 2, z: 4, core: 2. Of those that a mesh axis runs over, the one named last changes fastest.
Arguments:
- node_features: bfloat16 [4, 8192, 256], P('rep', 'dom'), may hold values from -32 to 32
- cotangent: bfloat16 [4, 8192, 256], P('rep', 'dom'), may hold values from -6 to 6
- w_qkv: bfloat16 [256, 768], replicated, may hold values from -0.375 to 0.375
- w_out: bfloat16 [256, 256], replicated, may hold values from -0.375 to 0.375
- w_up: bfloat16 [256, 512], replicated, may hold values from -0.375 to 0.375
- w_down: bfloat16 [512, 256], replicated, may hold values from -0.25 to 0.25
- tile_cols: int32 [4, 64, 8], P('rep'), may hold values from 0 to 63, as said below
- tile_count: int32 [4, 64], P('rep', 'dom'), may hold values from 1 to 9
- live: int32 [4, 8192], P('rep', 'dom'), may hold values 0 or 1
Outputs:
- layer_out: bfloat16 [4, 8192, 256], P('rep', 'dom')
- feature_grad: bfloat16 [4, 8192, 256], P('rep', 'dom')
- grad_qkv: float32 [256, 768], replicated
- grad_wout: float32 [256, 256], replicated
- grad_up: float32 [256, 512], replicated
- grad_down: float32 [512, 256], replicated
Inputs may be any that keep to these rules, and one draw needn't show every extreme that they name: `tile_cols`: within each aligned run of 8 row blocks, the 64 listed blocks are all different; at most 8 of them lie in any one aligned run of 8 blocks, and exactly 8 lie in some such run.
All inputs are finite; a program needn't handle non-finite values. No bound on the sum of `live` on one device may be relied on, other than what follows from the above.
Results may differ from a plain program's by a relative error of at most 0.015.
Values may be sent and summed in bfloat16 or wider, within the bound.
A program may use at most 192 MiB of HBM per device.

v0:
```python
import math

import jax
import jax.numpy as jnp
from jax import lax
from jax.sharding import PartitionSpec as P

HEADS = 8
BLOCK = 128
EXP = 8


NEG = -1e30


def split_heads(values):
    return values.reshape(values.shape[:-1] + (HEADS, values.shape[-1] // HEADS))


def allowed_keys(tile_ok, key_live, key_ids, query_ids):
    live_part = key_live[:, None, :, :] > 0.5
    self_part = key_ids[:, None, :, :] == query_ids[:, :, None, None]
    return tile_ok[:, None, :, None] & (live_part | self_part)


def probabilities(queries, keys, allowed, score_scale):
    scores = (
        jnp.einsum(
            "gqhd,gtkhd->ghqtk",
            split_heads(queries),
            split_heads(keys),
            preferred_element_type=jnp.float32,
        )
        * score_scale
    )
    scores = jnp.where(allowed[:, None], scores, NEG)
    largest = jnp.max(scores, axis=(3, 4), keepdims=True)
    weights = jnp.exp(scores - largest)
    total = jnp.sum(weights, axis=(3, 4), keepdims=True)
    return (weights / total).astype(jnp.bfloat16)


def attend_group(queries, kv_tiles, allowed, score_scale):
    width = queries.shape[-1]
    probs = probabilities(queries, kv_tiles[..., :width], allowed, score_scale)
    result = jnp.einsum(
        "ghqtk,gtkhd->gqhd",
        probs,
        split_heads(kv_tiles[..., width:]),
        preferred_element_type=jnp.float32,
    )
    return result.reshape(queries.shape)


def back_group(queries, kv_tiles, allowed, d_attended, attended32, score_scale):
    width = queries.shape[-1]
    keys = kv_tiles[..., :width]
    values = kv_tiles[..., width:]
    probs = probabilities(queries, keys, allowed, score_scale)
    d_heads = split_heads(d_attended)
    delta = jnp.transpose(
        jnp.sum(d_heads.astype(jnp.float32) * split_heads(attended32), axis=-1), (0, 2, 1)
    )
    d_probs = jnp.einsum(
        "gqhd,gtkhd->ghqtk", d_heads, split_heads(values), preferred_element_type=jnp.float32
    )
    d_scores = (
        probs.astype(jnp.float32) * (d_probs - delta[:, :, :, None, None]) * score_scale
    ).astype(jnp.bfloat16)
    d_queries = jnp.einsum(
        "ghqtk,gtkhd->gqhd", d_scores, split_heads(keys), preferred_element_type=jnp.float32
    )
    d_queries = d_queries.reshape(queries.shape).astype(jnp.bfloat16)
    d_keys = jnp.einsum(
        "ghqtk,gqhd->gtkhd", d_scores, split_heads(queries), preferred_element_type=jnp.float32
    )
    d_values = jnp.einsum("ghqtk,gqhd->gtkhd", probs, d_heads, preferred_element_type=jnp.float32)
    merged_shape = d_keys.shape[:3] + (width,)
    d_kv = jnp.concatenate([d_keys.reshape(merged_shape), d_values.reshape(merged_shape)], axis=-1)
    return (d_queries, d_kv[:, 0], d_kv[:, 1:].astype(jnp.bfloat16))


def local(node_features, cotangent, w_qkv, w_out, w_up, w_down, tile_cols, tile_count, live):
    features = node_features[0]
    grad_in = cotangent[0]
    rows_dev = features.shape[0]
    width = features.shape[1]
    blocks_dev = rows_dev // BLOCK
    dom_count = lax.axis_size("dom")
    own_index = lax.axis_index("dom")
    capacity = max(2, -(-(blocks_dev * EXP) // dom_count))
    score_scale = float(width // HEADS) ** (-0.5)
    group_size = math.gcd(blocks_dev, 4)
    group_count = blocks_dev // group_size
    qkv_rows = jnp.dot(features, w_qkv, preferred_element_type=jnp.float32).astype(jnp.bfloat16)
    queries = qkv_rows[:, :width].reshape(blocks_dev, BLOCK, width)
    kv_local = qkv_rows[:, width:].reshape(blocks_dev, BLOCK, 2 * width)
    live_local = live[0].astype(jnp.bfloat16).reshape(blocks_dev, BLOCK)
    ref_table = tile_cols[0].reshape(dom_count, blocks_dev * EXP)
    owner_dev = ref_table // blocks_dev
    same_owner = owner_dev[:, :, None] == owner_dev[:, None, :]
    smaller = ref_table[:, None, :] < ref_table[:, :, None]
    slot_rank = jnp.sum(same_owner & smaller, axis=2)
    my_refs = lax.dynamic_index_in_dim(ref_table, own_index, 0, keepdims=False)
    my_rank = lax.dynamic_index_in_dim(slot_rank, own_index, 0, keepdims=False)
    flat_slot = my_refs // blocks_dev * capacity + my_rank
    slot_ids = jnp.arange(capacity, dtype=jnp.int32)
    wanted = (slot_rank[:, :, None] == slot_ids[None, None, :]) & (owner_dev == own_index)[
        :, :, None
    ]
    local_block = ref_table - own_index * blocks_dev
    send_index = jnp.sum(jnp.where(wanted, local_block[:, :, None], 0), axis=1)

    def far_tiles(received, trailing):
        picked = received.reshape((dom_count * capacity,) + trailing)[flat_slot]
        return picked.reshape((blocks_dev, EXP) + trailing)

    feature_rows = features.reshape(blocks_dev, BLOCK, width)
    got_features, got_live = (
        lax.all_to_all(feature_rows[send_index], "dom", split_axis=0, concat_axis=0, tiled=True),
        lax.all_to_all(live_local[send_index], "dom", split_axis=0, concat_axis=0, tiled=True),
    )
    got_kv = jnp.dot(
        got_features.reshape(-1, width), w_qkv[:, width:], preferred_element_type=jnp.float32
    ).astype(jnp.bfloat16)
    got_kv = got_kv.reshape(dom_count, capacity, BLOCK, 2 * width)
    kv_tiles = jnp.concatenate([kv_local[:, None], far_tiles(got_kv, (BLOCK, 2 * width))], axis=1)
    live_tiles = jnp.concatenate([live_local[:, None], far_tiles(got_live, (BLOCK,))], axis=1)
    row_ids = jnp.arange(BLOCK, dtype=jnp.int32)
    own_blocks = own_index * blocks_dev + jnp.arange(blocks_dev, dtype=jnp.int32)
    tile_blocks = jnp.concatenate([own_blocks[:, None], my_refs.reshape(blocks_dev, EXP)], axis=1)
    key_ids = tile_blocks[:, :, None] * BLOCK + row_ids[None, None, :]
    query_ids = own_blocks[:, None] * BLOCK + row_ids[None, :]
    tile_ok = jnp.concatenate(
        [
            jnp.ones((blocks_dev, 1), bool),
            jnp.arange(EXP, dtype=jnp.int32)[None, :] < tile_count[0][:, None] - 1,
        ],
        axis=1,
    )
    allowed = allowed_keys(tile_ok, live_tiles, key_ids, query_ids)

    def grouped(values):
        return values.reshape((group_count, group_size) + values.shape[1:])

    attended32 = lax.map(
        lambda member: attend_group(member[0], member[1], member[2], score_scale),
        (grouped(queries), grouped(kv_tiles), grouped(allowed)),
    ).reshape(rows_dev, width)
    attended = attended32.astype(jnp.bfloat16)
    mixed = (
        features.astype(jnp.float32) + jnp.dot(attended, w_out, preferred_element_type=jnp.float32)
    ).astype(jnp.bfloat16)
    pre = jnp.dot(mixed, w_up, preferred_element_type=jnp.float32)
    act = jax.nn.silu(pre).astype(jnp.bfloat16)
    layer_out = (
        mixed.astype(jnp.float32) + jnp.dot(act, w_down, preferred_element_type=jnp.float32)
    ).astype(jnp.bfloat16)
    sigma = jax.nn.sigmoid(pre)
    d_act = (
        jnp.dot(grad_in, w_down.T, preferred_element_type=jnp.float32)
        * sigma
        * (1.0 + pre * (1.0 - sigma))
    ).astype(jnp.bfloat16)
    d_mixed = (
        grad_in.astype(jnp.float32) + jnp.dot(d_act, w_up.T, preferred_element_type=jnp.float32)
    ).astype(jnp.bfloat16)
    d_attended = jnp.dot(d_mixed, w_out.T, preferred_element_type=jnp.float32).astype(jnp.bfloat16)
    grad_wout = jnp.einsum("nd,ne->de", attended, d_mixed, preferred_element_type=jnp.float32)
    grad_up = jnp.einsum("nd,ne->de", mixed, d_act, preferred_element_type=jnp.float32)
    grad_down = jnp.einsum("nd,ne->de", act, grad_in, preferred_element_type=jnp.float32)
    d_queries, near_term, far_term = lax.map(
        lambda member: back_group(
            member[0], member[1], member[2], member[3], member[4], score_scale
        ),
        (
            grouped(queries),
            grouped(kv_tiles),
            grouped(allowed),
            grouped(d_attended.reshape(blocks_dev, BLOCK, width)),
            grouped(attended32.reshape(blocks_dev, BLOCK, width)),
        ),
    )
    send_back = jnp.zeros((dom_count * capacity, BLOCK, 2 * width), jnp.bfloat16)
    send_back = send_back.at[flat_slot].set(far_term.reshape(blocks_dev * EXP, BLOCK, 2 * width))
    got_back = lax.all_to_all(
        send_back.reshape(dom_count, capacity, BLOCK, 2 * width),
        "dom",
        split_axis=0,
        concat_axis=0,
        tiled=True,
    )
    summed = (
        jnp.zeros((blocks_dev, BLOCK, 2 * width), jnp.float32)
        .at[send_index.reshape(-1)]
        .add(got_back.reshape(dom_count * capacity, BLOCK, 2 * width).astype(jnp.float32))
    )
    d_kv = (
        (near_term.reshape(blocks_dev, BLOCK, 2 * width) + summed)
        .reshape(rows_dev, 2 * width)
        .astype(jnp.bfloat16)
    )
    d_qkv = jnp.concatenate([d_queries.reshape(rows_dev, width), d_kv], axis=1)
    feature_grad = (
        d_mixed.astype(jnp.float32) + jnp.dot(d_qkv, w_qkv.T, preferred_element_type=jnp.float32)
    ).astype(jnp.bfloat16)
    grad_qkv = jnp.einsum("nd,ne->de", features, d_qkv, preferred_element_type=jnp.float32)
    grad_qkv, grad_wout, grad_up, grad_down = lax.psum(
        (grad_qkv, grad_wout, grad_up, grad_down), ("dom", "rep")
    )
    factor = float(rows_dev * dom_count * lax.axis_size("rep")) ** (-0.5)
    return (
        layer_out[None],
        feature_grad[None],
        grad_qkv * factor,
        grad_wout * factor,
        grad_up * factor,
        grad_down * factor,
    )


def solution(mesh):
    return jax.shard_map(
        local,
        mesh=mesh,
        in_specs=(
            P("rep", "dom", None),
            P("rep", "dom", None),
            P(),
            P(),
            P(),
            P(),
            P("rep", None, None),
            P("rep", "dom"),
            P("rep", "dom"),
        ),
        out_specs=(P("rep", "dom", None), P("rep", "dom", None), P(), P(), P(), P()),
        check_vma=False,
    )
```

profile of v0, /device:TPU:0, one launch (start us, length us, event | category | flops | bytes accessed | tf_op | source)
XLA Modules:
  0.0 826.5 jit_solution(17677419289433717702)
XLA Ops:
  11.3 7.3 all-to-all-start.1
  18.6 3.8 gather_fusion
  22.4 2.8 all-to-all-done.1
  25.2 4.6 all-to-all-start
  34.0 5.9 or_and_fusion
  39.9 81.9 %all-to-all-done = bf16[8,8,128,256]{3,2,1,0:T(8,128)(2,1)} async-done(((bf16[8,8,128,256]{3,2,1,0:T(8,128)(2,1)}), bf16[8,8,128,256]{3,2,1,0:T(8,128)(2,1)}, u32[]{:S(2)}, u32[]{:S(2)}) %all-to-all-start) | async-done | bytes 4194336 | tf_op jit(solution)/shard_map/all_to_all | solution.py:120
  121.8 7.8 convolution_convert_fusion
  129.6 8.9 %gather_fusion.1 = bf16[64,128,512]{2,1,0:T(8,128)(2,1)} fusion(bf16[64,128,512]{2,1,0:T(8,128)(2,1)} %bitcast.229, s32[1024]{0:T(1024)S(1)} %pad_clamp_fusion), kind=kCustom, calls=%fused_computation.1 | custom fusion | bytes 16777472 | tf_op jit(solution)/shard_map/gather | solution.py:115
  138.5 11.9 %copy.86 = bf16[64,128,512]{1,2,0:T(8,128)(2,1)} copy(bf16[64,128,512]{2,1,0:T(8,128)(2,1)} %gather_fusion.1) | data formatting | bytes 16777216 | tf_op jit(solution)/shard_map/gather | solution.py:115
  150.5 7.9 pad_maximum_fusion.1
  158.4 67.7 %while.24 = (s32[]{:T(128)}, f32[2,4,128,256]{2,3,1,0:T(8,128)}, bf16[2,4,9,128,512]{3,4,2,1,0:T(8,128)(2,1)}, pred[2,4,128,9,128]{2,4,3,1,0:T(8,128)(4,1)}, bf16[2,4,128,256]{2,3,1,0:T(8,128)(2,1)}, /*index=5*/s32[]{:T(128)}) while((s32[]{:T(128)}, f32[2,4,128,256]{2,3,1,0:T(8,128)}, bf16[2,4,9,128,512]{3,4,2,1,0:T(8,128)(2,1)}, ...), condition=%wide.region_5.6_spmd, body=%wide.region_2.5_spmd.sunk | while | flops 660594688 | bytes 87704168 | solution.py:146
  159.8 2.6 dynamic-slice_bitcast_fusion.9
  163.6 8.6 %fusion.100 = (f32[4,8,128]{2,1,0:T(8,128)S(1)}, f32[4,8,128,9,128]{2,4,3,1,0:T(8,128)}) fusion(pred[4,128,9,128]{1,3,2,0:T(8,128)(4,1)S(1)} %dynamic-slice_bitcast_fusion.8, bf16[4,128,8,32,1]{1,3,4,2,0:T(8,128)(2,1)S(1)} %bitcast.231, bf16[4,9,128,8,32]{2,4,3,1,0:T(8,128)(2,1)S(1)} %bitcast.217), kind=kOutput, calls=%fused_computation.9.clone.1 | convolution fusion | flops 316141568 | bytes 22102016 | tf_op jit(solution)/shard_map/while/body/eval_jaxpr/gqhd,gtkhd->ghqtk/dot_general | solution.py:28
  172.1 10.4 %fusion.101 = f32[4,8,128]{2,1,0:T(8,128)S(1)} fusion(f32[4,8,128,9,128]{2,4,3,1,0:T(8,128)} %get-tuple-element.296, f32[4,8,128]{2,1,0:T(8,128)S(1)} %get-tuple-element.297, pred[4,128,9,128]{1,3,2,0:T(8,128)(4,1)S(1)} %dynamic-slice_bitcast_fusion.8), kind=kLoop, calls=%fused_computation.10.clone.1 | loop fusion | flops 18870272 | bytes 19496960 | tf_op jit(solution)/shard_map/while/body/eval_jaxpr/reduce_sum | solution.py:39
  182.6 8.9 %fusion.102 = f32[4,8,32,128,1]{3,2,4,1,0:T(8,128)S(1)} fusion(f32[4,8,128,9,128]{2,4,3,1,0:T(8,128)} %get-tuple-element.296, f32[4,8,128]{2,1,0:T(8,128)S(1)} %fusion.101, f32[4,8,128]{2,1,0:T(8,128)S(1)} %get-tuple-element.297, pred[4,128,9,128]{1,3,2,0:T(8,128)(4,1)S(1)} %dynamic-slice_bitcast_fusion.8, bf16[4,9,128,8,32]{2,4,3,1,0:T(8,128)(2,1)S(1)} %bitcast.226), kind=kOutput, calls=%fused_computation.11.clone.1 | convolution fusion | flops 325582848 | bytes 22380544 | tf_op jit(solution)/shard_map/while/body/eval_jaxpr/ghqtk,gtkhd->gqhd/dot_general | solution.py:46
  193.5 2.6 dynamic-slice_bitcast_fusion.9
  197.2 8.6 %fusion.100 = (f32[4,8,128]{2,1,0:T(8,128)S(1)}, f32[4,8,128,9,128]{2,4,3,1,0:T(8,128)}) fusion(pred[4,128,9,128]{1,3,2,0:T(8,128)(4,1)S(1)} %dynamic-slice_bitcast_fusion.8, bf16[4,128,8,32,1]{1,3,4,2,0:T(8,128)(2,1)S(1)} %bitcast.231, bf16[4,9,128,8,32]{2,4,3,1,0:T(8,128)(2,1)S(1)} %bitcast.217), kind=kOutput, calls=%fused_computation.9.clone.1 | convolution fusion | flops 316141568 | bytes 22102016 | tf_op jit(solution)/shard_map/while/body/eval_jaxpr/gqhd,gtkhd->ghqtk/dot_general | solution.py:28
  205.8 10.4 %fusion.101 = f32[4,8,128]{2,1,0:T(8,128)S(1)} fusion(f32[4,8,128,9,128]{2,4,3,1,0:T(8,128)} %get-tuple-element.296, f32[4,8,128]{2,1,0:T(8,128)S(1)} %get-tuple-element.297, pred[4,128,9,128]{1,3,2,0:T(8,128)(4,1)S(1)} %dynamic-slice_bitcast_fusion.8), kind=kLoop, calls=%fused_computation.10.clone.1 | loop fusion | flops 18870272 | bytes 19496960 | tf_op jit(solution)/shard_map/while/body/eval_jaxpr/reduce_sum | solution.py:39
  216.2 8.9 %fusion.102 = f32[4,8,32,128,1]{3,2,4,1,0:T(8,128)S(1)} fusion(f32[4,8,128,9,128]{2,4,3,1,0:T(8,128)} %get-tuple-element.296, f32[4,8,128]{2,1,0:T(8,128)S(1)} %fusion.101, f32[4,8,128]{2,1,0:T(8,128)S(1)} %get-tuple-element.297, pred[4,128,9,128]{1,3,2,0:T(8,128)(4,1)S(1)} %dynamic-slice_bitcast_fusion.8, bf16[4,9,128,8,32]{2,4,3,1,0:T(8,128)(2,1)S(1)} %bitcast.226), kind=kOutput, calls=%fused_computation.11.clone.1 | convolution fusion | flops 325582848 | bytes 22380544 | tf_op jit(solution)/shard_map/while/body/eval_jaxpr/ghqtk,gtkhd->gqhd/dot_general | solution.py:46
  234.1 192.0 %while.25 = (s32[]{:T(128)}, bf16[2,4,128,256]{3,2,1,0:T(8,128)(2,1)}, f32[2,4,128,512]{3,2,1,0:T(8,128)}, bf16[2,4,8,128,512]{4,3,2,1,0:T(8,128)(2,1)}, bf16[2,...) while((s32[]{:T(128)}, ...), condition=%wide.region_10.11_spmd, body=%wide.region_6.10_spmd.sunk | while | flops 1599328256 | bytes 329959232 | solution.py:172
  246.5 2.8 dynamic-slice_bitcast_fusion.11
  249.4 2.0 fusion.112
  252.9 8.6 %fusion.113 = (f32[4,8,128]{2,1,0:T(8,128)S(1)}, f32[4,8,128,9,128]{2,4,3,1,0:T(8,128)}) fusion(pred[4,128,9,128]{1,3,2,0:T(8,128)(4,1)S(1)} %dynamic-slice_bitcast_fusion.10, bf16[4,128,8,32,1]{1,3,4,2,0:T(8,128)(2,1)S(1)} %bitcast.219, bf16[4,9,128,8,32]{2,4,3,1,0:T(8,128)(2,1)S(1)} %bitcast.215), kind=kOutput, calls=%fused_computation.25.clone.1 | convolution fusion | flops 316141568 | bytes 22102016 | tf_op jit(solution)/shard_map/while/body/eval_jaxpr/gqhd,gtkhd->ghqtk/dot_general | solution.py:28
  261.5 10.4 %fusion.114 = f32[4,8,128]{2,1,0:T(8,128)S(1)} fusion(f32[4,8,128,9,128]{2,4,3,1,0:T(8,128)} %get-tuple-element.309, f32[4,8,128]{2,1,0:T(8,128)S(1)} %get-tuple-element.310, pred[4,128,9,128]{1,3,2,0:T(8,128)(4,1)S(1)} %dynamic-slice_bitcast_fusion.10), kind=kLoop, calls=%fused_computation.26.clone.1 | loop fusion | flops 18870272 | bytes 19496960 | tf_op jit(solution)/shard_map/while/body/eval_jaxpr/reduce_sum | solution.py:39
  271.9 11.5 %divide_convert_fusion.6 = bf16[4,8,128,9,128]{2,4,3,1,0:T(8,128)(2,1)} fusion(f32[4,8,128,9,128]{2,4,3,1,0:T(8,128)} %get-tuple-element.309, f32[4,8,128]{2,1,0:T(8,128)S(1)} %fusion.114, f32[4,8,128]{2,1,0:T(8,128)S(1)} %get-tuple-element.310, pred[4,128,9,128]{1,3,2,0:T(8,128)(4,1)S(1)} %dynamic-slice_bitcast_fusion.10), kind=kLoop, calls=%fused_computation.22.clone.1 | loop fusion | flops 23592960 | bytes 28934144 | tf_op jit(solution)/shard_map/while/body/eval_jaxpr/convert_element_type | solution.py:40
  285.8 7.3 multiply_convert_fusion.4
  293.1 3.3 convolution_bitcast_fusion.5
  296.7 2.8 copy.150
  299.5 5.8 convolution_bitcast_fusion.6
  305.9 2.4 copy-done.4
  309.3 2.6 fusion.117
  312.0 6.4 copy.153
  318.3 4.8 constant_dynamic-update-slice_fusion.11
  323.1 2.1 fusion.116
  325.2 2.7 copy.152
  327.9 2.3 constant_dynamic-update-slice_fusion.10
  330.2 5.3 fusion.115
  336.3 2.8 dynamic-slice_bitcast_fusion.11
  342.7 8.6 %fusion.113 = (f32[4,8,128]{2,1,0:T(8,128)S(1)}, f32[4,8,128,9,128]{2,4,3,1,0:T(8,128)}) fusion(pred[4,128,9,128]{1,3,2,0:T(8,128)(4,1)S(1)} %dynamic-slice_bitcast_fusion.10, bf16[4,128,8,32,1]{1,3,4,2,0:T(8,128)(2,1)S(1)} %bitcast.219, bf16[4,9,128,8,32]{2,4,3,1,0:T(8,128)(2,1)S(1)} %bitcast.215), kind=kOutput, calls=%fused_computation.25.clone.1 | convolution fusion | flops 316141568 | bytes 22102016 | tf_op jit(solution)/shard_map/while/body/eval_jaxpr/gqhd,gtkhd->ghqtk/dot_general | solution.py:28
  351.3 10.4 %fusion.114 = f32[4,8,128]{2,1,0:T(8,128)S(1)} fusion(f32[4,8,128,9,128]{2,4,3,1,0:T(8,128)} %get-tuple-element.309, f32[4,8,128]{2,1,0:T(8,128)S(1)} %get-tuple-element.310, pred[4,128,9,128]{1,3,2,0:T(8,128)(4,1)S(1)} %dynamic-slice_bitcast_fusion.10), kind=kLoop, calls=%fused_computation.26.clone.1 | loop fusion | flops 18870272 | bytes 19496960 | tf_op jit(solution)/shard_map/while/body/eval_jaxpr/reduce_sum | solution.py:39
  361.7 11.5 %divide_convert_fusion.6 = bf16[4,8,128,9,128]{2,4,3,1,0:T(8,128)(2,1)} fusion(f32[4,8,128,9,128]{2,4,3,1,0:T(8,128)} %get-tuple-element.309, f32[4,8,128]{2,1,0:T(8,128)S(1)} %fusion.114, f32[4,8,128]{2,1,0:T(8,128)S(1)} %get-tuple-element.310, pred[4,128,9,128]{1,3,2,0:T(8,128)(4,1)S(1)} %dynamic-slice_bitcast_fusion.10), kind=kLoop, calls=%fused_computation.22.clone.1 | loop fusion | flops 23592960 | bytes 28934144 | tf_op jit(solution)/shard_map/while/body/eval_jaxpr/convert_element_type | solution.py:40
  375.6 7.3 multiply_convert_fusion.4
  382.9 3.3 convolution_bitcast_fusion.5
  386.5 2.8 copy.150
  389.3 5.8 convolution_bitcast_fusion.6
  395.7 2.4 copy-done.4
  399.1 2.6 fusion.117
  401.8 6.4 copy.153
  408.1 4.7 constant_dynamic-update-slice_fusion.11
  412.8 2.1 fusion.116
  415.0 2.7 copy.152
  417.6 2.3 constant_dynamic-update-slice_fusion.10
  419.9 5.3 fusion.115
  426.1 4.3 broadcast_in_dim.108
  430.4 22.3 %scatter_fusion = bf16[64,128,512]{2,1,0:T(8,128)(2,1)} fusion(bf16[64,128,512]{2,1,0:T(8,128)(2,1)} %broadcast_in_dim.108, s32[64]{0:T(128)S(1)} %copy-done.34, bf16[64,128,512]{2,1,0:T(8,128)(2,1)} %bitcast.236), kind=kCustom, calls=%fused_computation.4 | custom fusion | bytes 25166080 | tf_op jit(solution)/shard_map/scatter | solution.py:185
  452.7 5.2 all-to-all-start.2
  460.4 2.5 fusion.31
  462.9 177.0 %all-to-all-done.2 = bf16[8,8,128,512]{3,2,1,0:T(8,128)(2,1)} async-done(((bf16[8,8,128,512]{3,2,1,0:T(8,128)(2,1)}), bf16[8,8,128,512]{3,2,1,0:T(8,128)(2,1)}, u32[]{:S(2)}, u32[]{:S(2)}) %all-to-all-start.2) | async-done | bytes 8388640 | tf_op jit(solution)/shard_map/all_to_all | solution.py:186
  639.9 11.7 %bitcast_convert_fusion = f32[64,128,512]{2,1,0:T(8,128)} fusion(bf16[8,8,128,512]{3,2,1,0:T(8,128)(2,1)} %all-to-all-done.2), kind=kLoop, calls=%fused_computation.54 | loop fusion | flops 4194304 | bytes 25165824 | tf_op jit(solution)/shard_map/convert_element_type | solution.py:196
  651.6 23.3 %scatter_fusion.1 = f32[8,128,512]{2,1,0:T(8,128)S(1)} fusion(f32[8,128,512]{2,1,0:T(8,128)S(1)} %bitcast.218, s32[64]{0:T(128)S(1)} %fusion.41, f32[64,128,512]{2,1,0:T(8,128)} %bitcast_convert_fusion), kind=kCustom, calls=%fused_computation.5 | custom fusion | flops 4194304 | bytes 50331904 | tf_op jit(solution)/shard_map/scatter-add | solution.py:196
  676.0 2.5 convolution_bitcast_fusion.2
  678.6 2.2 fusion.29
  680.8 2.8 fusion.30
  683.6 129.0 %all-reduce.4.cloned.1.call-done = (f32[256,768]{0,1:T(8,128)}, f32[256,256]{1,0:T(8,128)}, f32[256,512]{1,0:T(8,128)}, f32[512,256]{1,0:T(8,128)}) async-done(((f32[256,768]{0,1:T(8,128)}, f32[256,256]{1,0:T(8,128)}, f32[256,512]{1,0:T(8,128)}, f32[512,256]{1,0:T(8,128)}), (f32[256,768]{0,1:T(8,128)}, f32[256,256]{1,0:T(8,128)}, f32[256,512]{1,0:T(8,128)}, ...) | async-done | bytes 2097168 | tf_op jit(solution)/shard_map/psum | solution.py:208
  (172 shorter events, 48.1 us)
Async XLA Ops:
  7.2 221.8 %copy-start = (bf16[256,512]{1,0:T(8,128)(2,1)S(1)}, bf16[256,512]{1,0:T(8,128)(2,1)}, u32[]{:S(2)}) copy-start(bf16[256,512]{1,0:T(8,128)(2,1)} %param.17) | copy-start | bytes 786436
  8.7 0.6 copy-start.30
  11.3 13.8 %all-to-all-start.1 = ((bf16[8,8,128]{2,1,0:T(8,128)(2,1)}), bf16[8,8,128]{2,1,0:T(8,128)(2,1)S(1)}, u32[]{:S(2)}, u32[]{:S(2)}) async-start(bf16[8,8,128]{2,1,0:T(8,128)(2,1)} %bitcast.53), calls=%async_computation.1 | async-start | bytes 32768 | tf_op jit(solution)/shard_map/all_to_all | solution.py:121
  22.4 7.4 copy-start.32
  22.4 7.4 copy-start.8
  22.4 7.4 copy-start.21
  25.2 96.7 %all-to-all-start = ((bf16[8,8,128,256]{3,2,1,0:T(8,128)(2,1)}), bf16[8,8,128,256]{3,2,1,0:T(8,128)(2,1)}, u32[]{:S(2)}, u32[]{:S(2)}) async-start(bf16[8,8,128,256]{3,2,1,0:T(8,128)(2,1)} %bitcast.233), calls=%async_computation | async-start | bytes 8388608 | tf_op jit(solution)/shard_map/all_to_all | solution.py:120
  29.8 2.6 copy-start.35
  32.6 0.6 copy-start.33
  158.4 69.1 %copy-start.27 = (bf16[256,256]{1,0:T(8,128)(2,1)S(1)}, bf16[256,256]{1,0:T(8,128)(2,1)}, u32[]{:S(2)}) copy-start(bf16[256,256]{1,0:T(8,128)(2,1)} %param.16) | copy-start | bytes 393220
  162.5 1.0 copy-start.10
  196.1 1.0 copy-start.10
  227.5 3.3 copy-start.12
  229.0 1.7 copy-start.16
  229.0 1.7 copy-start.25
  229.0 1.7 copy-start.28
  230.7 3.4 copy-start.11
  231.7 2.4 copy-start.19
  232.2 0.8 copy-start.14
  251.4 10.1 %copy-start.5 = (bf16[4,9,128,256]{2,3,1,0:T(8,128)(2,1)}, bf16[4,9,128,256]{2,3,1,0:T(8,128)(2,1)S(1)}, u32[]{:S(2)}) copy-start(bf16[4,9,128,256]{2,3,1,0:T(8,128)(2,1)S(1)} %get-tuple-element.308) | copy-start | bytes 7077892 | tf_op jit(solution)/shard_map/while
  293.1 3.7 copy-start.2
  305.3 4.0 copy-start.3
  305.9 2.4 copy-start.4
  312.0 11.1 %slice-start = ((s8[4718592]{0:T(1024)(128)(4,1)}), s8[524288]{0:T(1024)(128)(4,1)S(1)}, s32[]{:S(2)}) async-start(s8[4718592]{0:T(1024)(128)(4,1)} %bitcast.210), calls=%async_computation.4 | async-start | bytes 1048576 | tf_op jit(solution)/shard_map/while
  318.3 4.8 slice-start.1
  325.2 5.0 copy-start.6
  341.2 10.1 %copy-start.5 = (bf16[4,9,128,256]{2,3,1,0:T(8,128)(2,1)}, bf16[4,9,128,256]{2,3,1,0:T(8,128)(2,1)S(1)}, u32[]{:S(2)}) copy-start(bf16[4,9,128,256]{2,3,1,0:T(8,128)(2,1)S(1)} %get-tuple-element.308) | copy-start | bytes 7077892 | tf_op jit(solution)/shard_map/while
  382.9 3.7 copy-start.2
  395.1 4.0 copy-start.3
  395.7 2.4 copy-start.4
  401.8 11.1 %slice-start = ((s8[4718592]{0:T(1024)(128)(4,1)}), s8[524288]{0:T(1024)(128)(4,1)S(1)}, s32[]{:S(2)}) async-start(s8[4718592]{0:T(1024)(128)(4,1)} %bitcast.210), calls=%async_computation.4 | async-start | bytes 1048576 | tf_op jit(solution)/shard_map/while
  408.1 4.7 slice-start.1
  415.0 5.0 copy-start.6
  426.1 4.3 copy-start.34
  452.7 5.3 copy-start.31
  452.7 5.4 copy-start.13
  452.7 5.4 copy-start.15
  452.7 6.5 copy-start.17
  452.7 6.5 copy-start.20
  452.7 7.7 copy-start.26
  452.7 187.2 %all-to-all-start.2 = ((bf16[8,8,128,512]{3,2,1,0:T(8,128)(2,1)}), bf16[8,8,128,512]{3,2,1,0:T(8,128)(2,1)}, u32[]{:S(2)}, u32[]{:S(2)}) async-start(bf16[8,8,128,512]{3,2,1,0:T(8,128)(2,1)} %bitcast.224), calls=%async_computation.2 | async-start | bytes 16777216 | tf_op jit(solution)/shard_map/all_to_all | solution.py:186
  457.9 354.6 %all-reduce.4.cloned.1.call-start = ((), (), s32[]{:S(2)}) async-start(), calls=%async_computation.3 | async-start | bytes 4194304 | tf_op jit(solution)/shard_map/psum | solution.py:208
  639.9 11.7 %copy-start.7 = (f32[2,4,128,512]{3,2,1,0:T(8,128)S(1)}, f32[2,4,128,512]{3,2,1,0:T(8,128)}, u32[]{:S(2)}) copy-start(f32[2,4,128,512]{3,2,1,0:T(8,128)} %get-tuple-element.84) | copy-start | bytes 6291460
  651.6 24.4 %copy-start.9 = (bf16[1,1024,256]{2,1,0:T(8,128)(2,1)S(1)}, bf16[1,1024,256]{2,1,0:T(8,128)(2,1)}, u32[]{:S(2)}) copy-start(bf16[1,1024,256]{2,1,0:T(8,128)(2,1)} %param.13) | copy-start | bytes 1572868
  675.0 1.0 copy-start.23
  675.0 3.5 copy-start.18
  675.0 3.5 copy-start.24
  675.1 5.8 copy-start.22
  678.6 140.9 %copy-start.1 = (bf16[256,512]{1,0:T(8,128)(2,1)S(1)}, bf16[256,512]{1,0:T(8,128)(2,1)}, u32[]{:S(2)}) copy-start(bf16[256,512]{1,0:T(8,128)(2,1)} %param.17) | copy-start | bytes 786436
  812.6 6.2 copy-start.29
Sparse Core Ops, SparseCore 0:
  678.7 133.8 all-reduce.3
where the time goes:
time: 829 us; the launch traced here: 827 us
  waiting for transfers between devices  391 us (47%)
  local copies, waits for them, and re-layouts  138 us (17%)
  other arithmetic  131 us (16%)
  matrix products  122 us (15%)
  starting transfers between devices  17.2 us (2%)
  between operations  14.7 us (2%)
  loops' own time  13.1 us (2%)
    all_to_all x1, waiting for transfers between devices, local(): lax.all_to_all(send_back.reshape(dom_count, capacity, BLOCK, 2 * width),...  177 us
    psum x1, waiting for transfers between devices, local(): lax.psum((grad_qkv, grad_wout, grad_up, grad_down), ('dom', 'rep'))  129 us
    all_to_all x1, waiting for transfers between devices, local(): lax.all_to_all(feature_rows[send_index], 'dom', split_axis=0, concat_axis...  81.9 us
    reduce_sum x4, other arithmetic, probabilities(): total = jnp.sum(weights, axis=(3, 4), keepdims=True)  41.7 us
    dot_general x4, matrix products, probabilities(): jnp.einsum('gqhd,gtkhd->ghqtk', split_heads(queries), split_heads(keys),...  34.3 us
    dynamic_update_slice x12, local copies, waits for them, and re-layouts, local(): lax.map(lambda member: back_group(member[0], member[1], member[2], member...  33.9 us
    scatter-add x1, other arithmetic, local(): summed = jnp.zeros((blocks_dev, BLOCK, 2 * width), jnp.float32).at[send_i...  23.3 us
    convert_element_type x2, other arithmetic, probabilities(): return (weights / total).astype(jnp.bfloat16)  23.1 us
  transfers between devices with their start and end apart: 4, of which 4 were waited for; matrix products, arithmetic and copies ran while one was open for 3% of the time, Pallas kernels for 0%

commit v1 on v0

v1 whole, which is shorter than its diff:
```python
import math

import jax
import jax.numpy as jnp
from jax import lax
from jax.experimental import pallas as pl
from jax.experimental.pallas import tpu as pltpu
from jax.sharding import PartitionSpec as P

HEADS = 8
BLOCK = 128
EXP = 8
TILES = EXP + 1
EXTRA = 16
PAIRS = HEADS // 2

F32 = jnp.float32
BF16 = jnp.bfloat16


def dot_nn(a, b):
    return lax.dot_general(a, b, (((1,), (0,)), ((), ())), preferred_element_type=F32)


def dot_nt(a, b):
    return lax.dot_general(a, b, (((1,), (1,)), ((), ())), preferred_element_type=F32)


def dot_tn(a, b):
    return lax.dot_general(a, b, (((0,), (0,)), ((), ())), preferred_element_type=F32)


def layer_kernel(
    row_s, slot_s, self_s, count_s,
    feat_ref, cot_ref, live_ref, gath_ref, glive_ref,
    wqkv_ref, wqkvt_ref, wout_ref, wup_ref, wdown_ref,
    out_ref, part_ref, near_ref, far_ref, gqkv_ref, gout_ref, gup_ref, gdown_ref,
    feat_s, k_s, v_s, kt_s, vt_s, bias_s, e_s, ds_s, qbd_s, dobd_s, att_s, dq_s, rl_s,
):
    b = pl.program_id(0)
    width = feat_ref.shape[1]
    hw = width // HEADS
    scale = float(hw) ** -0.5

    @pl.when(b == 0)
    def _():
        gqkv_ref[...] = jnp.zeros_like(gqkv_ref)
        gout_ref[...] = jnp.zeros_like(gout_ref)
        gup_ref[...] = jnp.zeros_like(gup_ref)
        gdown_ref[...] = jnp.zeros_like(gdown_ref)

    eye = (
        lax.broadcasted_iota(jnp.int32, (BLOCK, BLOCK), 0)
        == lax.broadcasted_iota(jnp.int32, (BLOCK, BLOCK), 1)
    ).astype(F32)
    feat = feat_ref[...]
    cot = cot_ref[...]
    feat_s[0:BLOCK, :] = feat
    bias_s[0:BLOCK, :] = (jnp.maximum(live_ref[...], eye) - 1.0) * 1e30
    for t in range(EXP):
        row = pl.multiple_of(row_s[b * EXP + t], 16)
        place = pl.multiple_of(slot_s[b * EXP + t] * BLOCK, BLOCK)
        active = (t + 1 < count_s[b]).astype(F32)
        mine = self_s[b * EXP + t].astype(F32)
        feat_s[(t + 1) * BLOCK:(t + 2) * BLOCK, :] = gath_ref[pl.ds(row, BLOCK), :]
        seen = jnp.maximum(glive_ref[pl.ds(place, BLOCK), :], eye * mine) * active
        bias_s[(t + 1) * BLOCK:(t + 2) * BLOCK, :] = (seen - 1.0) * 1e30

    feats = feat_s[...]
    k_s[...] = dot_nn(feats, wqkv_ref[:, width:2 * width]).astype(BF16)
    v_s[...] = dot_nn(feats, wqkv_ref[:, 2 * width:]).astype(BF16)
    kt_s[...] = dot_nt(wqkvt_ref[width:2 * width, :], feats).astype(BF16)
    vt_s[...] = dot_nt(wqkvt_ref[2 * width:, :], feats).astype(BF16)
    qt = (dot_nt(wqkvt_ref[0:width, :], feat) * (scale * math.log2(math.e))).astype(BF16)
    head_of_row = lax.broadcasted_iota(jnp.int32, (width, BLOCK), 0) // hw

    def diagonal(values, pair):
        left = jnp.where(head_of_row == 2 * pair, values, jnp.zeros_like(values))
        right = jnp.where(head_of_row == 2 * pair + 1, values, jnp.zeros_like(values))
        return jnp.concatenate([left, right], axis=1)

    qf = qt.astype(F32)
    for p in range(PAIRS):
        r = 2 * hw * p
        qbd = diagonal(qf, p).astype(BF16)
        qbd_s[p] = qbd
        bias = bias_s[...]
        scores = dot_nn(k_s[...], qbd) + jnp.concatenate([bias, bias], axis=1)
        top = jnp.max(scores, axis=0, keepdims=True)
        weights = jnp.exp2(scores - top)
        rl = 1.0 / jnp.sum(weights, axis=0, keepdims=True)
        rl_s[p] = jnp.broadcast_to(rl, (8, 2 * BLOCK))
        wb = weights.astype(BF16)
        e_s[p] = wb
        ot = dot_nn(vt_s[r:r + 2 * hw, :], wb) * rl
        att_s[r:r + hw, :] = ot[0:hw, 0:BLOCK]
        att_s[r + hw:r + 2 * hw, :] = ot[hw:2 * hw, BLOCK:]

    att_t = att_s[...]
    attended = att_t.T.astype(BF16)
    mixed = (feat.astype(F32) + dot_nn(attended, wout_ref[...])).astype(BF16)
    pre = dot_nn(mixed, wup_ref[...])
    sigma = jax.nn.sigmoid(pre)
    act = (pre * sigma).astype(BF16)
    out_ref[...] = (mixed.astype(F32) + dot_nn(act, wdown_ref[...])).astype(BF16)
    d_act = (dot_nt(cot, wdown_ref[...]) * sigma * (1.0 + pre * (1.0 - sigma))).astype(BF16)
    d_mixed = (cot.astype(F32) + dot_nt(d_act, wup_ref[...])).astype(BF16)
    d_att_t = dot_nt(wout_ref[...], d_mixed)
    gout_ref[...] += dot_tn(attended, d_mixed)
    gup_ref[...] += dot_tn(mixed, d_act)
    gdown_ref[...] += dot_tn(act, cot)

    for p in range(PAIRS):
        r = 2 * hw * p
        rl = rl_s[p][0:1, :]
        dobd32 = diagonal(d_att_t, p) * rl
        dobd = dobd32.astype(BF16)
        dobd_s[p] = dobd
        delta = jnp.sum(dobd32 * jnp.concatenate([att_t, att_t], axis=1), axis=0, keepdims=True)
        d_probs = dot_nn(v_s[...], dobd)
        ds = (e_s[p].astype(F32) * (d_probs - delta)).astype(BF16)
        ds_s[p] = ds
        dqt = dot_nn(kt_s[r:r + 2 * hw, :], ds) * scale
        dq_s[r:r + hw, :] = dqt[0:hw, 0:BLOCK]
        dq_s[r + hw:r + 2 * hw, :] = dqt[hw:2 * hw, BLOCK:]

    dq = dq_s[...].T.astype(BF16)
    gqkv_ref[:, 0:width] += dot_tn(feat, dq)
    part_ref[...] = d_mixed.astype(F32) + dot_nt(dq, wqkv_ref[:, 0:width])

    dk = dot_nt(ds_s[0], qbd_s[0])
    dv = dot_nt(e_s[0], dobd_s[0])
    for p in range(1, PAIRS):
        dk += dot_nt(ds_s[p], qbd_s[p])
        dv += dot_nt(e_s[p], dobd_s[p])
    dk = dk * math.log(2.0)
    near_ref[:, 0:width] = dk[0:BLOCK]
    near_ref[:, width:] = dv[0:BLOCK]
    dkb = dk.astype(BF16)
    dvb = dv.astype(BF16)
    for t in range(EXP):
        place = pl.multiple_of(slot_s[b * EXP + t] * BLOCK, BLOCK)
        far_ref[pl.ds(place, BLOCK), 0:width] = dkb[(t + 1) * BLOCK:(t + 2) * BLOCK]
        far_ref[pl.ds(place, BLOCK), width:] = dvb[(t + 1) * BLOCK:(t + 2) * BLOCK]
    gqkv_ref[:, width:2 * width] += dot_tn(feats, dkb)
    gqkv_ref[:, 2 * width:] += dot_tn(feats, dvb)


def run_layer(scalars, features, cot, live_col, gathered, glive_col, weights, slots):
    rows, width = features.shape
    w_qkv, w_qkv_t, w_out, w_up, w_down = weights
    hidden = w_up.shape[1]
    blocks = rows // BLOCK
    keys = TILES * BLOCK

    def by_block(cols):
        return pl.BlockSpec((BLOCK, cols), lambda b, *_: (b, 0))

    def whole(array):
        return pl.BlockSpec(array.shape, lambda b, *_: (0, 0))

    out_shape = [
        jax.ShapeDtypeStruct((rows, width), BF16),
        jax.ShapeDtypeStruct((rows, width), F32),
        jax.ShapeDtypeStruct((rows, 2 * width), F32),
        jax.ShapeDtypeStruct((slots * BLOCK, 2 * width), BF16),
        jax.ShapeDtypeStruct((width, 3 * width), F32),
        jax.ShapeDtypeStruct((width, width), F32),
        jax.ShapeDtypeStruct((width, hidden), F32),
        jax.ShapeDtypeStruct((hidden, width), F32),
    ]
    return pl.pallas_call(
        layer_kernel,
        out_shape=out_shape,
        grid_spec=pltpu.PrefetchScalarGridSpec(
            num_scalar_prefetch=4,
            grid=(blocks,),
            in_specs=[
                by_block(width), by_block(width), by_block(1),
                whole(gathered), whole(glive_col),
                whole(w_qkv), whole(w_qkv_t), whole(w_out), whole(w_up), whole(w_down),
            ],
            out_specs=[by_block(width), by_block(width), by_block(2 * width)]
            + [whole(s) for s in out_shape[3:]],
            scratch_shapes=[
                pltpu.VMEM((keys, width), BF16),
                pltpu.VMEM((keys, width), BF16),
                pltpu.VMEM((keys, width), BF16),
                pltpu.VMEM((width, keys), BF16),
                pltpu.VMEM((width, keys), BF16),
                pltpu.VMEM((keys, BLOCK), F32),
                pltpu.VMEM((PAIRS, keys, 2 * BLOCK), BF16),
                pltpu.VMEM((PAIRS, keys, 2 * BLOCK), BF16),
                pltpu.VMEM((PAIRS, width, 2 * BLOCK), BF16),
                pltpu.VMEM((PAIRS, width, 2 * BLOCK), BF16),
                pltpu.VMEM((width, BLOCK), F32),
                pltpu.VMEM((width, BLOCK), F32),
                pltpu.VMEM((PAIRS, 8, 2 * BLOCK), F32),
            ],
        ),
        compiler_params=pltpu.CompilerParams(
            dimension_semantics=("arbitrary",), vmem_limit_bytes=56 * 2**20
        ),
    )(*scalars, features, cot, live_col, gathered, glive_col, w_qkv, w_qkv_t, w_out, w_up, w_down)


def local(node_features, cotangent, w_qkv, w_out, w_up, w_down, tile_cols, tile_count, live):
    features = node_features[0]
    grad_in = cotangent[0]
    rows_dev, width = features.shape
    blocks_dev = rows_dev // BLOCK
    dom_count = lax.axis_size("dom")
    own_index = lax.axis_index("dom")
    capacity = max(2, -(-(blocks_dev * EXP) // dom_count))
    slots = dom_count * capacity
    everything = capacity == blocks_dev
    live_rows = capacity * BLOCK // width
    live_local = live[0].astype(BF16)
    table = tile_cols[0].reshape(dom_count, blocks_dev * EXP)
    my_refs = lax.dynamic_index_in_dim(table, own_index, 0, keepdims=False)

    def padded(values):
        return jnp.pad(values, ((0, 0),) * (values.ndim - 2) + ((0, EXTRA - live_rows), (0, 0)))

    if everything:
        slot = my_refs
        payload = jnp.concatenate(
            [features, padded(live_local.reshape(live_rows, width))], axis=0
        )
        got = lax.all_gather(payload, "dom", axis=0, tiled=False)
    else:
        owner_dev = table // blocks_dev
        same_owner = owner_dev[:, :, None] == owner_dev[:, None, :]
        smaller = table[:, None, :] < table[:, :, None]
        slot_rank = jnp.sum(same_owner & smaller, axis=2)
        my_rank = lax.dynamic_index_in_dim(slot_rank, own_index, 0, keepdims=False)
        slot = my_refs // blocks_dev * capacity + my_rank
        slot_ids = jnp.arange(capacity, dtype=jnp.int32)
        wanted = (slot_rank[:, :, None] == slot_ids[None, None, :]) & (owner_dev == own_index)[
            :, :, None
        ]
        local_block = table - own_index * blocks_dev
        send_index = jnp.sum(jnp.where(wanted, local_block[:, :, None], 0), axis=1)
        sent = features.reshape(blocks_dev, BLOCK, width)[send_index]
        sent_live = live_local.reshape(blocks_dev, BLOCK)[send_index]
        payload = jnp.concatenate(
            [
                sent.reshape(dom_count, capacity * BLOCK, width),
                padded(sent_live.reshape(dom_count, live_rows, width)),
            ],
            axis=1,
        )
        got = lax.all_to_all(payload, "dom", split_axis=0, concat_axis=0, tiled=True)
    stride = capacity * BLOCK + EXTRA
    glive_col = (
        got[:, capacity * BLOCK:capacity * BLOCK + live_rows, :]
        .reshape(slots * BLOCK, 1)
        .astype(F32)
    )
    row_at = slot // capacity * stride + slot % capacity * BLOCK
    own_block = own_index * blocks_dev + jnp.arange(blocks_dev * EXP, dtype=jnp.int32) // EXP
    mine = (my_refs == own_block).astype(jnp.int32)
    layer_out, part, near, far, g_qkv, g_out, g_up, g_down = run_layer(
        (row_at, slot, mine, tile_count[0]),
        features,
        grad_in,
        live[0].astype(F32).reshape(rows_dev, 1),
        got.reshape(dom_count * stride, width),
        glive_col,
        (w_qkv, w_qkv.T, w_out, w_up, w_down),
        slots,
    )
    if everything:
        summed = lax.psum_scatter(far, "dom", scatter_dimension=0, tiled=True).astype(F32)
    else:
        back = lax.all_to_all(
            far.reshape(dom_count, capacity, BLOCK, 2 * width),
            "dom",
            split_axis=0,
            concat_axis=0,
            tiled=True,
        )
        summed = (
            jnp.zeros((blocks_dev, BLOCK, 2 * width), F32)
            .at[send_index.reshape(-1)]
            .add(back.reshape(slots, BLOCK, 2 * width).astype(F32))
            .reshape(rows_dev, 2 * width)
        )
    grads = lax.psum((g_qkv, g_out, g_up, g_down), ("dom", "rep"))
    d_kv = (near + summed).astype(BF16)
    feature_grad = (part + dot_nt(d_kv, w_qkv[:, width:])).astype(BF16)
    factor = float(rows_dev * dom_count * lax.axis_size("rep")) ** (-0.5)
    return (layer_out[None], feature_grad[None]) + tuple(g * factor for g in grads)


def solution(mesh):
    return jax.shard_map(
        local,
        mesh=mesh,
        in_specs=(
            P("rep", "dom", None),
            P("rep", "dom", None),
            P(),
            P(),
            P(),
            P(),
            P("rep", None, None),
            P("rep", "dom"),
            P("rep", "dom"),
        ),
        out_specs=(P("rep", "dom", None), P("rep", "dom", None), P(), P(), P(), P()),
        check_vma=False,
    )
```

time: 829 us -> 466 us (0.56)
  local copies, waits for them, and re-layouts: 138 us -> 9.06 us
  matrix products: 122 us -> 2.49 us
  other arithmetic: 131 us -> 12.1 us
  Pallas kernels: 0 us -> 77.3 us
  waiting for transfers between devices: 391 us -> 350 us
  starting transfers between devices: 17.2 us -> 0.12 us
  loops' own time: 13.1 us -> 0 us
    all_to_all x3 -> x0, waiting for transfers between devices: 262 us -> none  [the longest x1 177 us: local(): lax.all_to_all(send_back.reshape(dom_count, capacity, BLOCK, 2 * width),...]
    reduce_scatter x0 -> x1, waiting for transfers between devices: none -> 145 us  [local(): lax.psum_scatter(far, 'dom', scatter_dimension=0, tiled=True).astype(F32)]
    dot_general x27 -> x1, matrix products: 122 us -> 2.49 us  [dot_nt(): lax.dot_general(a, b, (((1,), (1,)), ((), ())), preferred_element_type=F32)]
    pallas_call x0 -> x1, Pallas kernels: none -> 77.3 us  [run_layer(): pl.pallas_call(layer_kernel, out_shape=out_shape, grid_spec=pltpu.Prefetc...]
    all_gather x0 -> x1, waiting for transfers between devices: none -> 72.9 us  [local(): got = lax.all_gather(payload, 'dom', axis=0, tiled=False)]
    reduce_sum x8 -> x0, other arithmetic: 42.5 us -> none  [the longest x4 41.7 us: probabilities(): total = jnp.sum(weights, axis=(3, 4), keepdims=True)]
    dynamic_update_slice x14 -> x0, local copies, waits for them, and re-layouts: 35.6 us -> none  [the longest x12 33.9 us: local(): lax.map(lambda member: back_group(member[0], member[1], member[2], member...]
    convert_element_type x6 -> x4, other arithmetic: 35.6 us -> 2.01 us  [the longest x1 0.76 us: local(): glive_col = got[:, capacity * BLOCK:capacity * BLOCK + live_rows, :].resh...]
  transfers between devices with their start and end apart: 4 -> 3, of which waited for: 4 -> 3; matrix products, arithmetic and copies ran while one was open for 3% -> 3% of each run, Pallas kernels for 0% -> 0%
where the time goes in v1:
time: 466 us; the launch traced here: 465 us
  waiting for transfers between devices  350 us (75%)
  Pallas kernels  77.3 us (17%)
  between operations  13.8 us (3%)
  other arithmetic  12.1 us (3%)
  local copies, waits for them, and re-layouts  9.06 us (2%)
    reduce_scatter x1, waiting for transfers between devices, local(): lax.psum_scatter(far, 'dom', scatter_dimension=0, tiled=True).astype(F32)  145 us
    psum x1, waiting for transfers between devices, local(): grads = lax.psum((g_qkv, g_out, g_up, g_down), ('dom', 'rep'))  132 us
    pallas_call x1, Pallas kernels, run_layer(): pl.pallas_call(layer_kernel, out_shape=out_shape, grid_spec=pltpu.Prefetc...  77.3 us
    all_gather x1, waiting for transfers between devices, local(): got = lax.all_gather(payload, 'dom', axis=0, tiled=False)  72.9 us
  transfers between devices with their start and end apart: 3, of which 3 were waited for; matrix products, arithmetic and copies ran while one was open for 3% of the time, Pallas kernels for 0%

profile of v1, /device:TPU:0, one launch (start us, length us, event | category | flops | bytes accessed | tf_op | source)
XLA Modules:
  0.0 465.2 jit_solution(786716601385518869)
XLA Ops:
  7.2 0.0 copy-start.3
  7.2 0.0 all-gather.3.cloned.1.call-start
  7.2 0.7 convert_reduce_fusion
  8.0 1.9 fusion.3
  9.8 0.0 all-gather.3.cloned.1.call-update
  9.9 0.0 all-reduce.4.cloned.1.call-start
  9.9 0.8 copy.16
  10.7 0.1 reshape_squeeze.3
  10.8 1.9 copy.17
  12.7 0.0 copy-done.3
  12.7 1.0 copy.18.live_ref
  13.7 0.5 compare_convert_fusion
  14.2 0.0 copy-start.4
  14.2 0.5 fusion.7.row_s
  14.8 72.9 %all-gather.3.cloned.1.call-done.gath_ref = bf16[8320,256]{1,0:T(8,128)(2,1)} async-done(((bf16[1040,256]{1,0:T(8,128)(2,1)}), bf16[8320,256]{1,0:T(8,128)(2,1)}) %all-gather.3.cloned.1.call-update) | async-done | bytes 4259856 | tf_op jit(solution)/shard_map/all_gather | solution.py:230
  87.7 0.8 slice_convert_fusion
  88.5 5.2 %reshape.49.glive_ref = f32[8192,1]{1,0:T(8,128)} reshape(f32[8,4,256]{2,1,0:T(4,128)S(1)} %slice_convert_fusion) | data formatting | bytes 65536 | tf_op jit(solution)/shard_map/convert_element_type | solution.py:258
  93.7 0.0 copy-done.4
  93.7 77.3 %shard_map.136 = (bf16[1024,256]{1,0:T(8,128)(2,1)}, f32[1024,256]{1,0:T(8,128)}, f32[1024,512]{1,0:T(8,128)}, bf16[8192,512]{1,0:T(8,128)(2,1)}, f32[256,768]{1...) custom-call(s32[64]{0:T(128)} %fusion.7.row_s, s32[64]{0:T(128)} %copy-done.4, ...), custom_call_target="tpu_custom_call" | custom-call | tf_op jit(solution)/shard_map/pallas_call | solution.py:172
  171.0 0.0 all-reduce.4.cloned.1.call-update
  171.0 0.0 reduce-scatter.2.cloned.1.call-start
  171.1 0.7 reduce-scatter.2.cloned.1.call-update
  171.8 132.2 %all-reduce.4.cloned.1.call-done = (f32[256,768]{1,0:T(8,128)}, f32[256,256]{1,0:T(8,128)}, f32[256,512]{1,0:T(8,128)}, f32[512,256]{1,0:T(8,128)}) async-done(((f32[256,768]{1,0:T(8,128)}, f32[256,256]{1,0:T(8,128)}, f32[256,512]{1,0:T(8,128)}, f32[512,256]{1,0:T(8,128)}), (f32[256,768]{1,0:T(8,128)}, f32[256,256]{1,0:T(8,128)}, f32[256,512]{1,0:T(8,128)}, ...) | async-done | bytes 2097168 | tf_op jit(solution)/shard_map/psum | solution.py:289
  304.0 0.0 copy-start
  304.0 0.0 copy-start.1
  304.0 0.0 copy-start.2
  304.0 1.8 broadcast_multiply_fusion.3
  305.8 1.9 broadcast_multiply_fusion.2
  307.7 1.9 broadcast_multiply_fusion.1
  309.6 2.1 broadcast_multiply_fusion
  311.7 144.5 %reduce-scatter.2.cloned.1.call-done = bf16[1024,512]{1,0:T(8,128)(2,1)} async-done(((bf16[8192,512]{1,0:T(8,128)(2,1)}), bf16[1024,512]{1,0:T(8,128)(2,1)}) %reduce-scatter.2.cloned.1.call-update) | async-done | bytes 1048592 | tf_op jit(solution)/shard_map/reduce_scatter | solution.py:274
  456.2 0.0 copy-done
  456.2 0.0 copy-done.1
  456.2 0.0 copy-done.2
  456.2 2.5 fusion.1
  (2 shorter events, 0.0 us)
Async XLA Ops:
  7.2 5.5 %copy-start.3 = (s32[1,1024]{1,0:T(1,128)S(1)}, s32[1,1024]{1,0:T(1,128)}, u32[]{:S(2)}) copy-start(s32[1,1024]{1,0:T(1,128)} %param.17) | copy-start | bytes 12292
  7.2 80.5 %all-gather.3.cloned.1.call-start = ((), (), s32[]{:S(2)}) async-start(), calls=%async_computation.2 | async-start | bytes 4792320 | tf_op jit(solution)/shard_map/all_gather | solution.py:230
  9.9 294.1 %all-reduce.4.cloned.1.call-start = ((), (), s32[]{:S(2)}) async-start(), calls=%async_computation.3 | async-start | bytes 4194304 | tf_op jit(solution)/shard_map/psum | solution.py:289
  14.2 79.5 %copy-start.4 = (s32[64]{0:T(128)}, s32[64]{0:T(128)S(1)}, u32[]{:S(2)}) copy-start(s32[64]{0:T(128)S(1)} %get-tuple-element.27.slot_s) | copy-start | bytes 772
  171.0 285.2 %reduce-scatter.2.cloned.1.call-start = ((), (), s32[]{:S(2)}) async-start(), calls=%async_computation.1 | async-start | bytes 9437184 | tf_op jit(solution)/shard_map/reduce_scatter | solution.py:274
  304.0 152.2 %copy-start = (bf16[256,768]{1,0:T(8,128)(2,1)S(1)}, bf16[256,768]{1,0:T(8,128)(2,1)}, u32[]{:S(2)}) copy-start(bf16[256,768]{1,0:T(8,128)(2,1)} %wqkv_ref.1) | copy-start | bytes 1179652
  304.0 152.2 %copy-start.1 = (f32[1024,512]{1,0:T(8,128)S(1)}, f32[1024,512]{1,0:T(8,128)}, u32[]{:S(2)}) copy-start(f32[1024,512]{1,0:T(8,128)} %get-tuple-element.16) | copy-start | bytes 6291460
  304.0 152.2 %copy-start.2 = (f32[1024,256]{1,0:T(8,128)S(1)}, f32[1024,256]{1,0:T(8,128)}, u32[]{:S(2)}) copy-start(f32[1024,256]{1,0:T(8,128)} %get-tuple-element.15) | copy-start | bytes 3145732
Sparse Core Ops, SparseCore 0:
  10.8 76.8 all-gather.2
  171.1 132.7 all-reduce.3
  308.0 148.0 reduce-scatter.1

commit v2 on v1

--- a/solution.py
+++ b/solution.py
@@ -1,3 +1,4 @@
+import functools
 import math
 
 import jax
@@ -31,6 +32,7 @@
 
 
 def layer_kernel(
+    factor,
     row_s, slot_s, self_s, count_s,
     feat_ref, cot_ref, live_ref, gath_ref, glive_ref,
     wqkv_ref, wqkvt_ref, wout_ref, wup_ref, wdown_ref,
@@ -56,14 +58,17 @@
     feat = feat_ref[...]
     cot = cot_ref[...]
     feat_s[0:BLOCK, :] = feat
-    bias_s[0:BLOCK, :] = (jnp.maximum(live_ref[...], eye) - 1.0) * 1e30
+
+    def column(ref, index):
+        return jnp.sum(eye * ref[pl.ds(index, 1), :], axis=1, keepdims=True)
+
+    bias_s[0:BLOCK, :] = (jnp.maximum(column(live_ref, b), eye) - 1.0) * 1e30
     for t in range(EXP):
         row = pl.multiple_of(row_s[b * EXP + t], 16)
-        place = pl.multiple_of(slot_s[b * EXP + t] * BLOCK, BLOCK)
         active = (t + 1 < count_s[b]).astype(F32)
         mine = self_s[b * EXP + t].astype(F32)
         feat_s[(t + 1) * BLOCK:(t + 2) * BLOCK, :] = gath_ref[pl.ds(row, BLOCK), :]
-        seen = jnp.maximum(glive_ref[pl.ds(place, BLOCK), :], eye * mine) * active
+        seen = jnp.maximum(column(glive_ref, slot_s[b * EXP + t]), eye * mine) * active
         bias_s[(t + 1) * BLOCK:(t + 2) * BLOCK, :] = (seen - 1.0) * 1e30
 
     feats = feat_s[...]
@@ -145,8 +150,13 @@
     gqkv_ref[:, width:2 * width] += dot_tn(feats, dkb)
     gqkv_ref[:, 2 * width:] += dot_tn(feats, dvb)
 
-
-def run_layer(scalars, features, cot, live_col, gathered, glive_col, weights, slots):
+    @pl.when(b == pl.num_programs(0) - 1)
+    def _():
+        for ref in (gqkv_ref, gout_ref, gup_ref, gdown_ref):
+            ref[...] = ref[...] * factor
+
+
+def run_layer(scalars, features, cot, live_rows, gathered, glive_rows, weights, slots, factor):
     rows, width = features.shape
     w_qkv, w_qkv_t, w_out, w_up, w_down = weights
     hidden = w_up.shape[1]
@@ -170,14 +180,14 @@
         jax.ShapeDtypeStruct((hidden, width), F32),
     ]
     return pl.pallas_call(
-        layer_kernel,
+        functools.partial(layer_kernel, factor),
         out_shape=out_shape,
         grid_spec=pltpu.PrefetchScalarGridSpec(
             num_scalar_prefetch=4,
             grid=(blocks,),
             in_specs=[
-                by_block(width), by_block(width), by_block(1),
-                whole(gathered), whole(glive_col),
+                by_block(width), by_block(width), whole(live_rows),
+                whole(gathered), whole(glive_rows),
                 whole(w_qkv), whole(w_qkv_t), whole(w_out), whole(w_up), whole(w_down),
             ],
             out_specs=[by_block(width), by_block(width), by_block(2 * width)]
@@ -201,7 +211,7 @@
         compiler_params=pltpu.CompilerParams(
             dimension_semantics=("arbitrary",), vmem_limit_bytes=56 * 2**20
         ),
-    )(*scalars, features, cot, live_col, gathered, glive_col, w_qkv, w_qkv_t, w_out, w_up, w_down)
+    )(*scalars, features, cot, live_rows, gathered, glive_rows, w_qkv, w_qkv_t, w_out, w_up, w_down)
 
 
 def local(node_features, cotangent, w_qkv, w_out, w_up, w_down, tile_cols, tile_count, live):
@@ -214,18 +224,18 @@
     capacity = max(2, -(-(blocks_dev * EXP) // dom_count))
     slots = dom_count * capacity
     everything = capacity == blocks_dev
-    live_rows = capacity * BLOCK // width
+    packed = capacity * BLOCK // width
     live_local = live[0].astype(BF16)
     table = tile_cols[0].reshape(dom_count, blocks_dev * EXP)
     my_refs = lax.dynamic_index_in_dim(table, own_index, 0, keepdims=False)
 
     def padded(values):
-        return jnp.pad(values, ((0, 0),) * (values.ndim - 2) + ((0, EXTRA - live_rows), (0, 0)))
+        return jnp.pad(values, ((0, 0),) * (values.ndim - 2) + ((0, EXTRA - packed), (0, 0)))
 
     if everything:
         slot = my_refs
         payload = jnp.concatenate(
-            [features, padded(live_local.reshape(live_rows, width))], axis=0
+            [features, padded(live_local.reshape(packed, width))], axis=0
         )
         got = lax.all_gather(payload, "dom", axis=0, tiled=False)
     else:
@@ -246,32 +256,41 @@
         payload = jnp.concatenate(
             [
                 sent.reshape(dom_count, capacity * BLOCK, width),
-                padded(sent_live.reshape(dom_count, live_rows, width)),
+                padded(sent_live.reshape(dom_count, packed, width)),
             ],
             axis=1,
         )
         got = lax.all_to_all(payload, "dom", split_axis=0, concat_axis=0, tiled=True)
     stride = capacity * BLOCK + EXTRA
-    glive_col = (
-        got[:, capacity * BLOCK:capacity * BLOCK + live_rows, :]
-        .reshape(slots * BLOCK, 1)
+    glive_rows = (
+        got[:, capacity * BLOCK:capacity * BLOCK + packed, :]
+        .reshape(slots, BLOCK)
         .astype(F32)
     )
     row_at = slot // capacity * stride + slot % capacity * BLOCK
     own_block = own_index * blocks_dev + jnp.arange(blocks_dev * EXP, dtype=jnp.int32) // EXP
     mine = (my_refs == own_block).astype(jnp.int32)
+    factor = float(rows_dev * dom_count * lax.axis_size("rep")) ** (-0.5)
     layer_out, part, near, far, g_qkv, g_out, g_up, g_down = run_layer(
         (row_at, slot, mine, tile_count[0]),
         features,
         grad_in,
-        live[0].astype(F32).reshape(rows_dev, 1),
+        live[0].astype(F32).reshape(blocks_dev, BLOCK),
         got.reshape(dom_count * stride, width),
-        glive_col,
+        glive_rows,
         (w_qkv, w_qkv.T, w_out, w_up, w_down),
         slots,
+        factor,
     )
     if everything:
-        summed = lax.psum_scatter(far, "dom", scatter_dimension=0, tiled=True).astype(F32)
+        back = lax.all_to_all(
+            far.reshape(dom_count, rows_dev, 2 * width),
+            "dom",
+            split_axis=0,
+            concat_axis=0,
+            tiled=True,
+        )
+        summed = jnp.sum(back.astype(F32), axis=0)
     else:
         back = lax.all_to_all(
             far.reshape(dom_count, capacity, BLOCK, 2 * width),
@@ -289,8 +308,7 @@
     grads = lax.psum((g_qkv, g_out, g_up, g_down), ("dom", "rep"))
     d_kv = (near + summed).astype(BF16)
     feature_grad = (part + dot_nt(d_kv, w_qkv[:, width:])).astype(BF16)
-    factor = float(rows_dev * dom_count * lax.axis_size("rep")) ** (-0.5)
-    return (layer_out[None], feature_grad[None]) + tuple(g * factor for g in grads)
+    return (layer_out[None], feature_grad[None]) + tuple(grads)
 
 
 def solution(mesh):

time: 466 us -> 465 us (level)
  starting transfers between devices: 0.12 us -> 5.12 us
    all_to_all x0 -> x1, waiting for transfers between devices: none -> 194 us  [local(): lax.all_to_all(far.reshape(dom_count, rows_dev, 2 * width), 'dom', split_...]
    reduce_scatter x1 -> x0, waiting for transfers between devices: 145 us -> none  [local(): lax.psum_scatter(far, 'dom', scatter_dimension=0, tiled=True).astype(F32)]
    psum x1, waiting for transfers between devices: 132 us -> 80.9 us  [local(): grads = lax.psum((g_qkv, g_out, g_up, g_down), ('dom', 'rep'))]
    mul x4 -> x0, other arithmetic: 7.67 us -> none  [local(): g * factor]
    convert_element_type x2 -> x1, local copies, waits for them, and re-layouts: 6.27 us -> 0.62 us  [local(): glive_rows = got[:, capacity * BLOCK:capacity * BLOCK + packed, :].reshap...]
    unnamed x12 -> x18, local copies, waits for them, and re-layouts: 2.7 us -> 8.11 us
    all_to_all x0 -> x1, starting transfers between devices: none -> 5.04 us  [local(): lax.all_to_all(far.reshape(dom_count, rows_dev, 2 * width), 'dom', split_...]
    reduce_sum x0 -> x1, other arithmetic: none -> 4.86 us  [local(): summed = jnp.sum(back.astype(F32), axis=0)]
  transfers between devices with their start and end apart: 3 -> 3, of which waited for: 3 -> 3; matrix products, arithmetic and copies ran while one was open for 3% -> 2% of each run, Pallas kernels for 0% -> 0%
where the time goes in v2:
time: 465 us
  waiting for transfers between devices  348 us (75%)
  Pallas kernels  76.8 us (17%)
  between operations  14.1 us (3%)
  other arithmetic  10.7 us (2%)
  local copies, waits for them, and re-layouts  8.83 us (2%)
  starting transfers between devices  5.12 us (1%)
    all_to_all x1, waiting for transfers between devices, local(): lax.all_to_all(far.reshape(dom_count, rows_dev, 2 * width), 'dom', split_...  194 us
    psum x1, waiting for transfers between devices, local(): grads = lax.psum((g_qkv, g_out, g_up, g_down), ('dom', 'rep'))  80.9 us
    pallas_call x1, Pallas kernels, run_layer(): pl.pallas_call(functools.partial(layer_kernel, factor), out_shape=out_sha...  76.8 us
    all_gather x1, waiting for transfers between devices, local(): got = lax.all_gather(payload, 'dom', axis=0, tiled=False)  72.6 us
  transfers between devices with their start and end apart: 3, of which 3 were waited for; matrix products, arithmetic and copies ran while one was open for 2% of the time, Pallas kernels for 0%

profile of v2, /device:TPU:0, one launch (start us, length us, event | category | flops | bytes accessed | tf_op | source)
XLA Modules:
  0.0 464.6 jit_solution(3815840046075724527)
XLA Ops:
  7.2 0.0 all-gather.3.cloned.1.call-start
  7.2 0.7 convert_reduce_fusion.1
  7.9 1.9 fusion.3
  9.8 0.0 all-gather.3.cloned.1.call-update
  9.8 1.3 convert_element_type.34
  11.1 0.8 copy.16
  11.9 0.1 reshape_squeeze.3
  12.0 1.9 copy.17
  13.9 0.6 compare_convert_fusion
  14.5 0.0 copy-start.5
  14.5 0.6 fusion.7.row_s
  15.1 72.6 %all-gather.3.cloned.1.call-done.gath_ref = bf16[8320,256]{1,0:T(8,128)(2,1)} async-done(((bf16[1040,256]{1,0:T(8,128)(2,1)}), bf16[8320,256]{1,0:T(8,128)(2,1)}) %all-gather.3.cloned.1.call-update) | async-done | bytes 4259856 | tf_op jit(solution)/shard_map/all_gather | solution.py:240
  87.7 0.8 slice_convert_fusion
  88.4 0.6 reshape.29.glive_ref
  89.1 0.0 copy-done.5
  89.1 76.8 %shard_map.136 = (bf16[1024,256]{1,0:T(8,128)(2,1)}, f32[1024,256]{1,0:T(8,128)}, f32[1024,512]{1,0:T(8,128)}, bf16[8192,512]{1,0:T(8,128)(2,1)}, f32[256,768]{1...) custom-call(s32[64]{0:T(128)} %fusion.7.row_s, s32[64]{0:T(128)} %copy-done.5, ...), custom_call_target="tpu_custom_call" | custom-call | tf_op jit(solution)/shard_map/pallas_call | solution.py:182
  165.9 5.0 %all-to-all-start = ((bf16[8,1024,512]{2,1,0:T(8,128)(2,1)}), bf16[8,1024,512]{2,1,0:T(8,128)(2,1)}, u32[]{:S(2)}, u32[]{:S(2)}) async-start(bf16[8,1024,512]{2,1,0:T(8,128)(2,1)} %bitcast.13), calls=%async_computation | async-start | bytes 16777216 | tf_op jit(solution)/shard_map/all_to_all | solution.py:286
  170.9 0.0 all-reduce.4.cloned.1.call-start
  171.0 0.7 all-reduce.4.cloned.1.call-update
  171.7 0.0 copy-start
  171.7 0.0 copy-start.1
  171.7 0.0 copy-start.2
  171.7 193.5 %all-to-all-done = bf16[8,1024,512]{2,1,0:T(8,128)(2,1)} async-done(((bf16[8,1024,512]{2,1,0:T(8,128)(2,1)}), bf16[8,1024,512]{2,1,0:T(8,128)(2,1)}, u32[]{:S(2)}, u32[]{:S(2)}) %all-to-all-start) | async-done | bytes 8388640 | tf_op jit(solution)/shard_map/all_to_all | solution.py:286
  365.2 4.9 %convert_reduce_fusion = f32[1024,512]{1,0:T(8,128)S(1)} fusion(bf16[8,1024,512]{2,1,0:T(8,128)(2,1)} %all-to-all-done), kind=kLoop, calls=%fused_computation | loop fusion | flops 7864320 | bytes 10485760 | tf_op jit(solution)/shard_map/reduce_sum | solution.py:293
  370.1 0.0 copy-done
  370.1 0.0 copy-done.1
  370.1 0.0 copy-done.2
  370.1 1.4 fusion.1
  371.5 80.9 %all-reduce.4.cloned.1.call-done = (f32[256,768]{1,0:T(8,128)}, f32[256,256]{1,0:T(8,128)}, f32[256,512]{1,0:T(8,128)}, f32[512,256]{1,0:T(8,128)}) async-done(((f32[256,768]{1,0:T(8,128)}, f32[256,256]{1,0:T(8,128)}, f32[256,512]{1,0:T(8,128)}, f32[512,256]{1,0:T(8,128)}), (f32[256,768]{1,0:T(8,128)}, f32[256,256]{1,0:T(8,128)}, f32[256,512]{1,0:T(8,128)}, ...) | async-done | bytes 2097168 | tf_op jit(solution)/shard_map/psum | solution.py:308
  452.4 0.0 copy-start.4
  452.4 0.0 copy-start.3
  452.4 2.2 copy.22
  454.5 1.7 copy.23
  456.2 0.0 copy-done.4
  456.2 0.8 copy.24
  457.0 0.0 copy-done.3
  457.0 0.8 copy.25
  (1 shorter events, 0.0 us)
Async XLA Ops:
  7.2 80.5 %all-gather.3.cloned.1.call-start = ((), (), s32[]{:S(2)}) async-start(), calls=%async_computation.1 | async-start | bytes 4792320 | tf_op jit(solution)/shard_map/all_gather | solution.py:240
  14.5 74.6 %copy-start.5 = (s32[64]{0:T(128)}, s32[64]{0:T(128)S(1)}, u32[]{:S(2)}) copy-start(s32[64]{0:T(128)S(1)} %get-tuple-element.27.slot_s) | copy-start | bytes 772
  165.9 199.3 %all-to-all-start = ((bf16[8,1024,512]{2,1,0:T(8,128)(2,1)}), bf16[8,1024,512]{2,1,0:T(8,128)(2,1)}, u32[]{:S(2)}, u32[]{:S(2)}) async-start(bf16[8,1024,512]{2,1,0:T(8,128)(2,1)} %bitcast.13), calls=%async_computation | async-start | bytes 16777216 | tf_op jit(solution)/shard_map/all_to_all | solution.py:286
  170.9 281.4 %all-reduce.4.cloned.1.call-start = ((), (), s32[]{:S(2)}) async-start(), calls=%async_computation.2 | async-start | bytes 4194304 | tf_op jit(solution)/shard_map/psum | solution.py:308
  171.7 198.4 %copy-start = (bf16[256,768]{1,0:T(8,128)(2,1)S(1)}, bf16[256,768]{1,0:T(8,128)(2,1)}, u32[]{:S(2)}) copy-start(bf16[256,768]{1,0:T(8,128)(2,1)} %wqkv_ref.1) | copy-start | bytes 1179652
  171.7 198.4 %copy-start.1 = (f32[1024,512]{1,0:T(8,128)S(1)}, f32[1024,512]{1,0:T(8,128)}, u32[]{:S(2)}) copy-start(f32[1024,512]{1,0:T(8,128)} %get-tuple-element.16) | copy-start | bytes 6291460
  171.7 198.4 %copy-start.2 = (f32[1024,256]{1,0:T(8,128)S(1)}, f32[1024,256]{1,0:T(8,128)}, u32[]{:S(2)}) copy-start(f32[1024,256]{1,0:T(8,128)} %get-tuple-element.15) | copy-start | bytes 3145732
  452.4 3.8 copy-start.4
  452.4 4.6 copy-start.3
Sparse Core Ops, SparseCore 0:
  10.8 76.8 all-gather.2
  178.0 274.2 all-reduce.3

commit v3 on v2

--- a/solution.py
+++ b/solution.py
@@ -305,10 +305,12 @@
             .add(back.reshape(slots, BLOCK, 2 * width).astype(F32))
             .reshape(rows_dev, 2 * width)
         )
-    grads = lax.psum((g_qkv, g_out, g_up, g_down), ("dom", "rep"))
+    grads = lax.psum(
+        tuple(g.astype(BF16) for g in (g_qkv, g_out, g_up, g_down)), ("dom", "rep")
+    )
     d_kv = (near + summed).astype(BF16)
     feature_grad = (part + dot_nt(d_kv, w_qkv[:, width:])).astype(BF16)
-    return (layer_out[None], feature_grad[None]) + tuple(grads)
+    return (layer_out[None], feature_grad[None]) + tuple(g.astype(F32) for g in grads)
 
 
 def solution(mesh):

time: 465 us -> 464 us (level)
  other arithmetic: 10.7 us -> 19.9 us
  local copies, waits for them, and re-layouts: 8.83 us -> 3.45 us
  waiting for transfers between devices: 348 us -> 343 us
    all_to_all x1, waiting for transfers between devices: 194 us -> 0.01 us  [local(): lax.all_to_all(far.reshape(dom_count, rows_dev, 2 * width), 'dom', split_...]
    psum x1, waiting for transfers between devices: 80.9 us -> 270 us  [local(): lax.psum(tuple((g.astype(BF16) for g in (g_qkv, g_out, g_up, g_down))), (...]
    convert_element_type x0 -> x8, other arithmetic: none -> 9.14 us  [the longest x4 6.22 us: local(): g.astype(F32)]
    unnamed x18 -> x20, local copies, waits for them, and re-layouts: 8.11 us -> 2.73 us
  transfers between devices with their start and end apart: 3 -> 3, of which waited for: 3 -> 2; matrix products, arithmetic and copies ran while one was open for 2% -> 3% of each run, Pallas kernels for 0% -> 0%
where the time goes in v3:
time: 464 us
  waiting for transfers between devices  343 us (74%)
  Pallas kernels  76.8 us (17%)
  other arithmetic  19.9 us (4%)
  between operations  14.1 us (3%)
  starting transfers between devices  5.25 us (1%)
    psum x1, waiting for transfers between devices, local(): lax.psum(tuple((g.astype(BF16) for g in (g_qkv, g_out, g_up, g_down))), (...  270 us
    pallas_call x1, Pallas kernels, run_layer(): pl.pallas_call(functools.partial(layer_kernel, factor), out_shape=out_sha...  76.8 us
    all_gather x1, waiting for transfers between devices, local(): got = lax.all_gather(payload, 'dom', axis=0, tiled=False)  72.7 us
  transfers between devices with their start and end apart: 3, of which 2 were waited for; matrix products, arithmetic and copies ran while one was open for 3% of the time, Pallas kernels for 0%

profile of v3, /device:TPU:0, one launch (start us, length us, event | category | flops | bytes accessed | tf_op | source)
XLA Modules:
  0.0 463.8 jit_solution(17767072791836108222)
XLA Ops:
  7.2 0.0 all-gather.3.cloned.1.call-start
  7.2 0.7 convert_reduce_fusion.1
  7.9 1.9 fusion.3
  9.8 0.0 all-gather.3.cloned.1.call-update
  9.8 1.3 convert_element_type.58
  11.1 0.8 copy.16
  11.9 0.1 reshape_squeeze.3
  12.0 1.9 copy.17
  13.9 0.6 compare_convert_fusion
  14.5 0.0 copy-start.8
  14.5 0.5 fusion.7.row_s
  15.0 72.7 %all-gather.3.cloned.1.call-done.gath_ref = bf16[8320,256]{1,0:T(8,128)(2,1)} async-done(((bf16[1040,256]{1,0:T(8,128)(2,1)}), bf16[8320,256]{1,0:T(8,128)(2,1)}) %all-gather.3.cloned.1.call-update) | async-done | bytes 4259856 | tf_op jit(solution)/shard_map/all_gather | solution.py:240
  87.7 0.8 slice_convert_fusion
  88.4 0.6 reshape.29.glive_ref
  89.1 0.0 copy-done.8
  89.1 76.8 %shard_map.136 = (bf16[1024,256]{1,0:T(8,128)(2,1)}, f32[1024,256]{1,0:T(8,128)}, f32[1024,512]{1,0:T(8,128)}, bf16[8192,512]{1,0:T(8,128)(2,1)}, f32[256,768]{1...) custom-call(s32[64]{0:T(128)} %fusion.7.row_s, s32[64]{0:T(128)} %copy-done.8, ...), custom_call_target="tpu_custom_call" | custom-call | tf_op jit(solution)/shard_map/pallas_call | solution.py:182
  165.9 0.0 copy-start.7
  165.9 0.0 copy-start.5
  165.9 0.0 copy-start.4
  166.0 5.2 %all-to-all-start = ((bf16[8,1024,512]{2,1,0:T(8,128)(2,1)}), bf16[8,1024,512]{2,1,0:T(8,128)(2,1)}, u32[]{:S(2)}, u32[]{:S(2)}) async-start(bf16[8,1024,512]{2,1,0:T(8,128)(2,1)} %bitcast.13), calls=%async_computation | async-start | bytes 16777216 | tf_op jit(solution)/shard_map/all_to_all | solution.py:286
  171.1 0.0 copy-start.3
  171.1 0.0 all-reduce.4.cloned.1.call-start
  171.2 0.0 copy-done.7
  171.2 0.7 convert_element_type.69
  171.9 0.0 copy-done.5
  171.9 0.7 convert_element_type.71
  172.6 0.0 copy-done.4
  172.6 0.7 convert_element_type.73
  173.3 0.0 copy-done.3
  173.4 0.8 convert_element_type.67
  174.1 0.0 all-reduce.4.cloned.1.call-update
  174.2 270.2 %all-reduce.4.cloned.1.call-done = (bf16[256,768]{1,0:T(8,128)(2,1)}, bf16[256,256]{1,0:T(8,128)(2,1)}, bf16[256,512]{1,0:T(8,128)(2,1)}, bf16[512,256]{1,0:T(8,128)(2,1)}) async-done(((bf16[256,768]{1,0:T(8,128)(2,1)}, bf16[256,256]{1,0:T(8,128)(2,1)}, bf16[256,512]{1,0:T(8,128)(2,1)}, bf16[512,256]{1,0:T(8,128)(2,1)}), (bf16[256,768]{1,0:T(8,128)(2,1)}, bf16[256,256]{1,0:T(8,128)(2,1)}, ...) | async-done | bytes 1048592 | tf_op jit(solution)/shard_map/psum | solution.py:308
  444.3 0.0 copy-start.6
  444.3 1.7 convert_element_type.70
  446.0 1.9 convert_element_type.68
  447.9 1.8 convert_element_type.72
  449.7 0.0 copy-done.6
  449.7 0.8 convert_element_type.74
  450.6 0.0 copy-start
  450.6 0.0 copy-start.1
  450.6 0.0 copy-start.2
  450.6 0.0 all-to-all-done
  450.6 5.0 %convert_reduce_fusion = f32[1024,512]{1,0:T(8,128)S(1)} fusion(bf16[8,1024,512]{2,1,0:T(8,128)(2,1)} %all-to-all-done), kind=kLoop, calls=%fused_computation | loop fusion | flops 7864320 | bytes 10485760 | tf_op jit(solution)/shard_map/reduce_sum | solution.py:293
  455.6 0.0 copy-done
  455.6 0.0 copy-done.1
  455.6 0.0 copy-done.2
  455.6 1.4 fusion.1
  (1 shorter events, 0.0 us)
Async XLA Ops:
  7.2 80.5 %all-gather.3.cloned.1.call-start = ((), (), s32[]{:S(2)}) async-start(), calls=%async_computation.1 | async-start | bytes 4792320 | tf_op jit(solution)/shard_map/all_gather | solution.py:240
  14.5 74.6 %copy-start.8 = (s32[64]{0:T(128)}, s32[64]{0:T(128)S(1)}, u32[]{:S(2)}) copy-start(s32[64]{0:T(128)S(1)} %get-tuple-element.27.slot_s) | copy-start | bytes 772
  165.9 5.3 %copy-start.7 = (f32[256,256]{1,0:T(8,128)S(1)}, f32[256,256]{1,0:T(8,128)}, u32[]{:S(2)}) copy-start(f32[256,256]{1,0:T(8,128)} %get-tuple-element.19) | copy-start | bytes 786436
  165.9 6.0 %copy-start.5 = (f32[256,512]{1,0:T(8,128)S(1)}, f32[256,512]{1,0:T(8,128)}, u32[]{:S(2)}) copy-start(f32[256,512]{1,0:T(8,128)} %get-tuple-element.20) | copy-start | bytes 1572868
  165.9 6.7 %copy-start.4 = (f32[512,256]{1,0:T(8,128)S(1)}, f32[512,256]{1,0:T(8,128)}, u32[]{:S(2)}) copy-start(f32[512,256]{1,0:T(8,128)} %get-tuple-element.21) | copy-start | bytes 1572868
  166.0 284.6 %all-to-all-start = ((bf16[8,1024,512]{2,1,0:T(8,128)(2,1)}), bf16[8,1024,512]{2,1,0:T(8,128)(2,1)}, u32[]{:S(2)}, u32[]{:S(2)}) async-start(bf16[8,1024,512]{2,1,0:T(8,128)(2,1)} %bitcast.13), calls=%async_computation | async-start | bytes 16777216 | tf_op jit(solution)/shard_map/all_to_all | solution.py:286
  171.1 2.2 copy-start.3
  171.1 273.2 %all-reduce.4.cloned.1.call-start = ((), (), s32[]{:S(2)}) async-start(), calls=%async_computation.2 | async-start | bytes 2097152 | tf_op jit(solution)/shard_map/psum | solution.py:308
  444.3 5.4 %copy-start.6 = (bf16[512,256]{1,0:T(8,128)(2,1)S(1)}, bf16[512,256]{1,0:T(8,128)(2,1)}, u32[]{:S(2)}) copy-start(bf16[512,256]{1,0:T(8,128)(2,1)} %get-tuple-element.25) | copy-start | bytes 786436
  450.6 5.0 %copy-start = (bf16[256,768]{1,0:T(8,128)(2,1)S(1)}, bf16[256,768]{1,0:T(8,128)(2,1)}, u32[]{:S(2)}) copy-start(bf16[256,768]{1,0:T(8,128)(2,1)} %wqkv_ref.1) | copy-start | bytes 1179652
  450.6 5.0 %copy-start.1 = (f32[1024,512]{1,0:T(8,128)S(1)}, f32[1024,512]{1,0:T(8,128)}, u32[]{:S(2)}) copy-start(f32[1024,512]{1,0:T(8,128)} %get-tuple-element.16) | copy-start | bytes 6291460
  450.6 5.0 %copy-start.2 = (f32[1024,256]{1,0:T(8,128)S(1)}, f32[1024,256]{1,0:T(8,128)}, u32[]{:S(2)}) copy-start(f32[1024,256]{1,0:T(8,128)} %get-tuple-element.15) | copy-start | bytes 3145732
Sparse Core Ops, SparseCore 0:
  10.8 76.8 all-gather.2
  178.1 266.2 all-reduce.3
